TPU v7x, 256 devices: a whole 4x4x8 slice. The times are simulated.
256 devices in a mesh: dp: 8 (over z_lo, x), seq: 32 (over z_hi, y, core).
Axes of the slice: x: 4, y: 4, z: 8 (z_hi: 4, z_lo: 2; z = z_hi * 2 + z_lo), core: 2. Of those that a mesh axis runs over, the one named last changes fastest.
Arguments:
- query: bfloat16 [8, 4096, 2048], P('dp', 'seq'), may hold values from -5 to 5
- keys: bfloat16 [8, 4096, 1024], P('dp', 'seq'), may hold values from -5 to 5
- values: bfloat16 [8, 4096, 1024], P('dp', 'seq'), may hold values from -6 to 6
- out_weight: bfloat16 [2048, 1920], P('dp'), may hold values from -0.125 to 0.125
- out_grad: bfloat16 [8, 4096, 1920], P('dp', 'seq'), may hold values from -6 to 6
- doc_blocks: int32 [8, 8], P('dp'), may hold values from 1 to 8, 32 in all within a row
Outputs:
- layer_out: bfloat16 [8, 4096, 1920], P('dp', 'seq')
- query_grad: bfloat16 [8, 4096, 2048], P('dp', 'seq')
- key_gradient: bfloat16 [8, 4096, 1024], P('dp', 'seq')
- value_gradient: bfloat16 [8, 4096, 1024], P('dp', 'seq')
- weight_grad: float32 [2048, 1920], P(('dp', 'seq'))
Inputs may be any that keep to these rules, and one draw needn't show every extreme that they name: `doc_blocks`: each row holds the lengths, in blocks of 128 tokens, of 8 documents that fill the sequence's 32 blocks; the longest has exactly 8 blocks.
All inputs are finite; a program needn't handle non-finite values.
Results may differ from a plain program's by a relative error of at most 0.02.
Values may be sent and summed in bfloat16 or wider, within the bound.
A program may use at most 192 MiB of HBM per device.

v0:
```python
import jax
import jax.numpy as jnp
from jax import lax
from jax.sharding import PartitionSpec as P

QUERY_HEADS = 8
KEY_VALUE_HEADS = 4
HEAD_SIZE = 256
WINDOW_TOKENS = 1024
BLOCK_TOKENS = 128


def from_behind(value, axis, steps):
    count = lax.axis_size(axis)
    leading, last = (max(0, -steps), min(count, count - steps))
    return lax.ppermute(value, axis, [(source, source + steps) for source in range(leading, last)])


def document_of(places, starts):
    return jnp.sum((starts[None, :] <= places[:, None]).astype(jnp.int32), axis=1) - 1


def per_device(query, keys, values, out_weight, out_grad, doc_blocks):
    token_positions = query.shape[1]
    group_total = QUERY_HEADS // KEY_VALUE_HEADS
    scale = HEAD_SIZE ** (-0.5)
    ahead = WINDOW_TOKENS // token_positions
    diagonal_rows = WINDOW_TOKENS + token_positions
    seq_index = lax.axis_index("seq")
    first = seq_index * token_positions
    pairs = jnp.stack([keys[0], values[0]])
    weight_full = lax.all_gather(out_weight, "dp", axis=0, tiled=True)
    blocks = [from_behind(pairs, "seq", distance) for distance in range(ahead, 0, -1)]
    widened_rows = jnp.concatenate(blocks + [pairs], axis=1)
    key_diagonal = widened_rows[0].reshape(diagonal_rows, KEY_VALUE_HEADS, HEAD_SIZE)
    value_diagonal = widened_rows[1].reshape(diagonal_rows, KEY_VALUE_HEADS, HEAD_SIZE)
    query_head_rows = query[0].reshape(token_positions, KEY_VALUE_HEADS, group_total, HEAD_SIZE)
    lengths = doc_blocks[0]
    starts = (jnp.cumsum(lengths) - lengths) * BLOCK_TOKENS
    query_place = first + jnp.arange(token_positions, dtype=jnp.int32)
    key_place = first - WINDOW_TOKENS + jnp.arange(diagonal_rows, dtype=jnp.int32)
    query_doc = document_of(query_place, starts)
    key_doc = document_of(key_place, starts)
    allowed = (key_place[None, :] <= query_place[:, None]) & (
        key_place[None, :] > query_place[:, None] - WINDOW_TOKENS
    )
    allowed = allowed & (key_doc[None, :] == query_doc[:, None])
    scores = (
        jnp.einsum(
            "tkgd,ekd->kgte", query_head_rows, key_diagonal, preferred_element_type=jnp.float32
        )
        * scale
    )
    masked = jnp.where(allowed, scores, -jnp.inf)
    top = jnp.max(masked, axis=-1, keepdims=True)
    lifted = jnp.where(allowed, jnp.exp(scores - top), 0.0)
    shares = lifted / jnp.sum(lifted, axis=-1, keepdims=True)
    shares_low = shares.astype(jnp.bfloat16)
    attn = jnp.einsum(
        "kgte,ekd->tkgd", shares_low, value_diagonal, preferred_element_type=jnp.float32
    )
    attn = attn.astype(jnp.bfloat16).reshape(token_positions, QUERY_HEADS * HEAD_SIZE)
    layer_out = jnp.dot(attn, weight_full, preferred_element_type=jnp.float32).astype(jnp.bfloat16)
    attention_gradient = lax.dot_general(
        out_grad[0], weight_full, (((1,), (1,)), ((), ())), preferred_element_type=jnp.float32
    )
    head_gradient = attention_gradient.astype(jnp.bfloat16).reshape(
        token_positions, KEY_VALUE_HEADS, group_total, HEAD_SIZE
    )
    grad_shares = jnp.einsum(
        "tkgd,ekd->kgte", head_gradient, value_diagonal, preferred_element_type=jnp.float32
    )
    centre = jnp.sum(shares * grad_shares, axis=-1, keepdims=True)
    grad_scores = (shares * (grad_shares - centre) * scale).astype(jnp.bfloat16)
    query_grad = jnp.einsum(
        "kgte,ekd->tkgd", grad_scores, key_diagonal, preferred_element_type=jnp.float32
    )
    query_grad = query_grad.astype(jnp.bfloat16).reshape(token_positions, QUERY_HEADS * HEAD_SIZE)
    key_portion = jnp.einsum(
        "kgte,tkgd->ekd", grad_scores, query_head_rows, preferred_element_type=jnp.float32
    )
    value_portion = jnp.einsum(
        "kgte,tkgd->ekd", shares_low, head_gradient, preferred_element_type=jnp.float32
    )
    parts = jnp.stack(
        [
            key_portion.reshape(diagonal_rows, KEY_VALUE_HEADS * HEAD_SIZE),
            value_portion.reshape(diagonal_rows, KEY_VALUE_HEADS * HEAD_SIZE),
        ]
    )
    owned = parts[:, WINDOW_TOKENS:]
    for distance in range(1, ahead + 1):
        piece = parts[
            :,
            WINDOW_TOKENS
            - distance * token_positions : WINDOW_TOKENS
            - (distance - 1) * token_positions,
        ]
        owned = owned + from_behind(piece, "seq", -distance)
    key_gradient = owned[0].astype(jnp.bfloat16)
    value_gradient = owned[1].astype(jnp.bfloat16)
    data_count = lax.axis_size("dp")
    seq_count = lax.axis_size("seq")
    normaliser = (data_count * seq_count * token_positions) ** (-0.5)
    grad_rows = out_grad[0]
    block = lax.psum_scatter(
        lax.dot_general(
            attn, grad_rows, (((0,), (0,)), ((), ())), preferred_element_type=jnp.float32
        ),
        "dp",
        scatter_dimension=0,
        tiled=True,
    )
    summed = lax.psum_scatter(block, "seq", scatter_dimension=0, tiled=True)
    weight_grad = summed * normaliser
    return (
        layer_out[None],
        query_grad[None],
        key_gradient[None],
        value_gradient[None],
        weight_grad,
    )


def solution(mesh):
    in_specs = (
        P("dp", "seq", None),
        P("dp", "seq", None),
        P("dp", "seq", None),
        P("dp", None),
        P("dp", "seq", None),
        P("dp", None),
    )
    out_specs = (
        P("dp", "seq", None),
        P("dp", "seq", None),
        P("dp", "seq", None),
        P("dp", "seq", None),
        P(("dp", "seq"), None),
    )
    return jax.shard_map(
        per_device, mesh=mesh, in_specs=in_specs, out_specs=out_specs, check_vma=False
    )
```

profile of v0, /device:TPU:1, one launch (start us, length us, event | category | flops | bytes accessed | tf_op | source)
XLA Modules:
  0.0 942.4 jit_solution(7204712861239313684)
XLA Ops:
  10.3 6.5 collective-permute-start
  16.8 7.0 collective-permute-start.1
  23.8 4.7 collective-permute-start.2
  28.4 2.1 collective-permute-start.3
  30.5 4.5 collective-permute-start.4
  38.9 2.9 collective-permute-start.5
  43.0 3.2 collective-permute-done.1
  46.2 7.7 collective-permute-start.6
  55.1 5.8 collective-permute-done.2
  60.9 20.3 %collective-permute-start.7 = (bf16[2,128,1024]{1,2,0:T(8,128)(2,1)S(1)}, bf16[2,128,1024]{1,2,0:T(8,128)(2,1)S(1)}, u32[]{:S(2)}, u32[]{:S(2)}) collective-permute-start(bf16[2,128,1024]{1,2,0:T(8,128)(2,1)S(1)} %pad_maximum_fusion.1), channel_id=1, source_target_pairs={{0,1},{1,2},{2,3},{3,4},{4,5},{5,6},{6,7},{7,8},{8,9},{9,10},{10,1... | collective-permute-start | bytes 1572872 | tf_op jit(solution)/shard_map/ppermute | solution.py:16
  83.0 4.4 collective-permute-done.7
  93.1 7.6 fusion.40
  101.0 6.1 all-gather.2.cloned.1.call-done
  107.1 6.7 convolution_convert_fusion
  113.7 2.1 copy.85
  115.8 4.9 fusion.51
  120.7 10.2 %fusion.12 = f32[4,1152,256,1]{1,2,3,0:T(8,128)} fusion(bf16[128,4,2,256]{0,3,2,1:T(8,128)(2,1)} %bitcast.101, f32[4,1152,128,2]{2,1,3,0:T(8,128)} %fusion.51, f32[4,2,128,1152]{2,3,1,0:T(8,128)} %copy-done.3, f32[4,2,128]{2,1,0:T(2,128)S(1)} %get-tuple-element.37), kind=kOutput, calls=%fused_computation.30 | convolution fusion | flops 612239488 | bytes 14684160 | tf_op jit(solution)/shard_map/kgte,tkgd->ekd/dot_general | solution.py:79
  131.0 6.0 copy.67
  137.0 5.5 fusion.20
  142.5 6.1 copy.68
  148.6 6.0 fusion.33
  158.5 332.3 %reduce-scatter.2.cloned.1.call-done = f32[256,1920]{1,0:T(8,128)} async-done(((f32[2048,1920]{1,0:T(8,128)}), f32[256,1920]{1,0:T(8,128)}) %reduce-scatter.2.cloned.1.call-update) | async-done | bytes 1966096 | tf_op jit(solution)/shard_map/reduce_scatter | solution.py:106
  496.1 2.5 collective-permute-start.8
  499.8 8.8 fusion.19
  508.6 2.1 copy.69
  510.7 5.5 fusion.18
  516.2 35.7 %collective-permute-done.11 = f32[2,128,1024]{2,1,0:T(8,128)} collective-permute-done((f32[2,128,1024]{2,1,0:T(8,128)}, f32[2,128,1024]{2,1,0:T(8,128)}, u32[]{:S(2)}, u32[]{:S(2)}) %collective-permute-start.11) | collective-permute-done | bytes 1048608 | tf_op jit(solution)/shard_map/ppermute | solution.py:16
  551.9 2.2 collective-permute-done.10
  554.1 10.0 %collective-permute-done.9 = f32[2,128,1024]{2,1,0:T(8,128)} collective-permute-done((f32[2,128,1024]{2,1,0:T(8,128)}, f32[2,128,1024]{2,1,0:T(8,128)}, u32[]{:S(2)}, u32[]{:S(2)}) %collective-permute-start.9) | collective-permute-done | bytes 1048608 | tf_op jit(solution)/shard_map/ppermute | solution.py:16
  564.1 2.5 collective-permute-done.8
  566.6 4.5 fusion.39
  571.9 362.5 %all-reduce.3.cloned.1.call-done = f32[256,1920]{1,0:T(8,128)} async-done(((f32[256,1920]{1,0:T(8,128)}), f32[256,1920]{1,0:T(8,128)}) %all-reduce.3.cloned.1.call-update) | async-done | bytes 1966096
  (68 shorter events, 28.7 us)
Async XLA Ops:
  7.2 85.9 %copy-start = (bf16[1,128,1920]{2,1,0:T(8,128)(2,1)S(1)}, bf16[1,128,1920]{2,1,0:T(8,128)(2,1)}, u32[]{:S(2)}) copy-start(bf16[1,128,1920]{2,1,0:T(8,128)(2,1)} %param.10) | copy-start | bytes 1474564
  7.2 99.9 %all-gather.2.cloned.1.call-start = ((), (), s32[]{:S(2)}) async-start(), calls=%async_computation.1 | async-start | bytes 8847360 | tf_op jit(solution)/shard_map/all_gather | solution.py:32
  7.9 482.9 %reduce-scatter.2.cloned.1.call-start = ((), (), s32[]{:S(2)}) async-start(), calls=%async_computation.2 | async-start | bytes 17694720 | tf_op jit(solution)/shard_map/reduce_scatter | solution.py:106
  10.3 28.7 %collective-permute-start = (bf16[2,128,1024]{1,2,0:T(8,128)(2,1)S(1)}, bf16[2,128,1024]{1,2,0:T(8,128)(2,1)}, u32[]{:S(2)}, u32[]{:S(2)}) collective-permute-start(bf16[2,128,1024]{1,2,0:T(8,128)(2,1)S(1)} %pad_maximum_fusion.1), channel_id=1, source_target_pairs={{0,8},{1,9},{2,10},{3,11},{4,12},{5,13},{6,14},{7,15},{8,16},{9,17... | collective-permute-start | bytes 1572872 | tf_op jit(solution)/shard_map/ppermute | solution.py:16
  16.8 29.4 %collective-permute-start.1 = (bf16[2,128,1024]{1,2,0:T(8,128)(2,1)S(1)}, bf16[2,128,1024]{1,2,0:T(8,128)(2,1)}, u32[]{:S(2)}, u32[]{:S(2)}) collective-permute-start(bf16[2,128,1024]{1,2,0:T(8,128)(2,1)S(1)} %pad_maximum_fusion.1), channel_id=1, source_target_pairs={{0,7},{1,8},{2,9},{3,10},{4,11},{5,12},{6,13},{7,14},{8,15},{9,16}... | collective-permute-start | bytes 1572872 | tf_op jit(solution)/shard_map/ppermute | solution.py:16
  23.8 37.1 %collective-permute-start.2 = (bf16[2,128,1024]{1,2,0:T(8,128)(2,1)S(1)}, bf16[2,128,1024]{1,2,0:T(8,128)(2,1)}, u32[]{:S(2)}, u32[]{:S(2)}) collective-permute-start(bf16[2,128,1024]{1,2,0:T(8,128)(2,1)S(1)} %pad_maximum_fusion.1), channel_id=1, source_target_pairs={{0,6},{1,7},{2,8},{3,9},{4,10},{5,11},{6,12},{7,13},{8,14},{9,15},... | collective-permute-start | bytes 1572872 | tf_op jit(solution)/shard_map/ppermute | solution.py:16
  28.4 53.9 %collective-permute-start.3 = (bf16[2,128,1024]{1,2,0:T(8,128)(2,1)S(1)}, bf16[2,128,1024]{1,2,0:T(8,128)(2,1)S(1)}, u32[]{:S(2)}, u32[]{:S(2)}) collective-permute-start(bf16[2,128,1024]{1,2,0:T(8,128)(2,1)S(1)} %pad_maximum_fusion.1), channel_id=1, source_target_pairs={{0,5},{1,6},{2,7},{3,8},{4,9},{5,10},{6,11},{7,12},{8,13},{9,14},{... | collective-permute-start | bytes 1572872 | tf_op jit(solution)/shard_map/ppermute | solution.py:16
  30.5 52.0 %collective-permute-start.4 = (bf16[2,128,1024]{1,2,0:T(8,128)(2,1)S(1)}, bf16[2,128,1024]{1,2,0:T(8,128)(2,1)S(1)}, u32[]{:S(2)}, u32[]{:S(2)}) collective-permute-start(bf16[2,128,1024]{1,2,0:T(8,128)(2,1)S(1)} %pad_maximum_fusion.1), channel_id=1, source_target_pairs={{0,4},{1,5},{2,6},{3,7},{4,8},{5,9},{6,10},{7,11},{8,12},{9,13},{1... | collective-permute-start | bytes 1572872 | tf_op jit(solution)/shard_map/ppermute | solution.py:16
  38.9 49.0 %copy-start.4 = (bf16[1,128,2048]{1,2,0:T(8,128)(2,1)}, bf16[1,128,2048]{1,2,0:T(8,128)(2,1)S(1)}, u32[]{:S(2)}) copy-start(bf16[1,128,2048]{1,2,0:T(8,128)(2,1)S(1)} %copy.84) | copy-start | bytes 1572868
  38.9 43.7 %collective-permute-start.5 = (bf16[2,128,1024]{1,2,0:T(8,128)(2,1)S(1)}, bf16[2,128,1024]{1,2,0:T(8,128)(2,1)S(1)}, u32[]{:S(2)}, u32[]{:S(2)}) collective-permute-start(bf16[2,128,1024]{1,2,0:T(8,128)(2,1)S(1)} %pad_maximum_fusion.1), channel_id=1, source_target_pairs={{0,3},{1,4},{2,5},{3,6},{4,7},{5,8},{6,9},{7,10},{8,11},{9,12},{10... | collective-permute-start | bytes 1572872 | tf_op jit(solution)/shard_map/ppermute | solution.py:16
  46.2 36.6 %collective-permute-start.6 = (bf16[2,128,1024]{1,2,0:T(8,128)(2,1)S(1)}, bf16[2,128,1024]{1,2,0:T(8,128)(2,1)S(1)}, u32[]{:S(2)}, u32[]{:S(2)}) collective-permute-start(bf16[2,128,1024]{1,2,0:T(8,128)(2,1)S(1)} %pad_maximum_fusion.1), channel_id=1, source_target_pairs={{0,2},{1,3},{2,4},{3,5},{4,6},{5,7},{6,8},{7,9},{8,10},{9,11},{10,... | collective-permute-start | bytes 1572872 | tf_op jit(solution)/shard_map/ppermute | solution.py:16
  60.9 26.4 %collective-permute-start.7 = (bf16[2,128,1024]{1,2,0:T(8,128)(2,1)S(1)}, bf16[2,128,1024]{1,2,0:T(8,128)(2,1)S(1)}, u32[]{:S(2)}, u32[]{:S(2)}) collective-permute-start(bf16[2,128,1024]{1,2,0:T(8,128)(2,1)S(1)} %pad_maximum_fusion.1), channel_id=1, source_target_pairs={{0,1},{1,2},{2,3},{3,4},{4,5},{5,6},{6,7},{7,8},{8,9},{9,10},{10,1... | collective-permute-start | bytes 1572872 | tf_op jit(solution)/shard_map/ppermute | solution.py:16
  87.9 3.0 copy-start.2
  90.9 2.1 copy-start.3
  100.7 833.7 %all-reduce.3.cloned.1.call-start = ((), (), s32[]{:S(2)}) async-start(), calls=%async_computation.3 | async-start | bytes 3932160
  148.6 350.0 %copy-start.5 = (u32[256]{0:T(256)S(1)}, u32[256]{0:T(256)}, u32[]{:S(2)}) copy-start(u32[256]{0:T(256)} %constant.37) | copy-start | bytes 3076
  154.6 338.8 %collective-permute-start.15 = (f32[2,128,1024]{2,1,0:T(8,128)}, f32[2,128,1024]{2,1,0:T(8,128)}, u32[]{:S(2)}, u32[]{:S(2)}) collective-permute-start(f32[2,128,1024]{2,1,0:T(8,128)} %get-tuple-element.31), channel_id=1, source_target_pairs={{8,0},{9,1},{10,2},{11,3},{12,4},{13,5},{14,6},{15,7},{16,8},{17,9... | collective-permute-start | bytes 3145736 | tf_op jit(solution)/shard_map/ppermute | solution.py:16
  155.9 338.8 %collective-permute-start.14 = (f32[2,128,1024]{2,1,0:T(8,128)}, f32[2,128,1024]{2,1,0:T(8,128)}, u32[]{:S(2)}, u32[]{:S(2)}) collective-permute-start(f32[2,128,1024]{2,1,0:T(8,128)} %get-tuple-element.32), channel_id=1, source_target_pairs={{7,0},{8,1},{9,2},{10,3},{11,4},{12,5},{13,6},{14,7},{15,8},{16,9}... | collective-permute-start | bytes 3145736 | tf_op jit(solution)/shard_map/ppermute | solution.py:16
  157.2 338.8 %collective-permute-start.13 = (f32[2,128,1024]{2,1,0:T(8,128)}, f32[2,128,1024]{2,1,0:T(8,128)}, u32[]{:S(2)}, u32[]{:S(2)}) collective-permute-start(f32[2,128,1024]{2,1,0:T(8,128)} %get-tuple-element.30), channel_id=1, source_target_pairs={{6,0},{7,1},{8,2},{9,3},{10,4},{11,5},{12,6},{13,7},{14,8},{15,9},... | collective-permute-start | bytes 3145736 | tf_op jit(solution)/shard_map/ppermute | solution.py:16
  490.8 25.3 %collective-permute-start.12 = (f32[2,128,1024]{2,1,0:T(8,128)}, f32[2,128,1024]{2,1,0:T(8,128)}, u32[]{:S(2)}, u32[]{:S(2)}) collective-permute-start(f32[2,128,1024]{2,1,0:T(8,128)} %get-tuple-element.29), channel_id=1, source_target_pairs={{5,0},{6,1},{7,2},{8,3},{9,4},{10,5},{11,6},{12,7},{13,8},{14,9},{... | collective-permute-start | bytes 3145736 | tf_op jit(solution)/shard_map/ppermute | solution.py:16
  492.1 59.8 %collective-permute-start.11 = (f32[2,128,1024]{2,1,0:T(8,128)}, f32[2,128,1024]{2,1,0:T(8,128)}, u32[]{:S(2)}, u32[]{:S(2)}) collective-permute-start(f32[2,128,1024]{2,1,0:T(8,128)} %get-tuple-element.28), channel_id=1, source_target_pairs={{4,0},{5,1},{6,2},{7,3},{8,4},{9,5},{10,6},{11,7},{12,8},{13,9},{1... | collective-permute-start | bytes 3145736 | tf_op jit(solution)/shard_map/ppermute | solution.py:16
  493.4 60.6 %collective-permute-start.10 = (f32[2,128,1024]{2,1,0:T(8,128)}, f32[2,128,1024]{2,1,0:T(8,128)}, u32[]{:S(2)}, u32[]{:S(2)}) collective-permute-start(f32[2,128,1024]{2,1,0:T(8,128)} %get-tuple-element.27), channel_id=1, source_target_pairs={{3,0},{4,1},{5,2},{6,3},{7,4},{8,5},{9,6},{10,7},{11,8},{12,9},{13... | collective-permute-start | bytes 3145736 | tf_op jit(solution)/shard_map/ppermute | solution.py:16
  494.8 69.3 %collective-permute-start.9 = (f32[2,128,1024]{2,1,0:T(8,128)}, f32[2,128,1024]{2,1,0:T(8,128)}, u32[]{:S(2)}, u32[]{:S(2)}) collective-permute-start(f32[2,128,1024]{2,1,0:T(8,128)} %get-tuple-element.26), channel_id=1, source_target_pairs={{2,0},{3,1},{4,2},{5,3},{6,4},{7,5},{8,6},{9,7},{10,8},{11,9},{12,... | collective-permute-start | bytes 3145736 | tf_op jit(solution)/shard_map/ppermute | solution.py:16
  496.1 70.6 %collective-permute-start.8 = (f32[2,128,1024]{2,1,0:T(8,128)}, f32[2,128,1024]{2,1,0:T(8,128)}, u32[]{:S(2)}, u32[]{:S(2)}) collective-permute-start(f32[2,128,1024]{2,1,0:T(8,128)} %get-tuple-element.25), channel_id=1, source_target_pairs={{1,0},{2,1},{3,2},{4,3},{5,4},{6,5},{7,6},{8,7},{9,8},{10,9},{11,1... | collective-permute-start | bytes 3145736 | tf_op jit(solution)/shard_map/ppermute | solution.py:16
  508.6 58.0 %slice-start = ((s8[4718592]{0:T(1024)(128)(4,1)}), s8[524288]{0:T(1024)(128)(4,1)S(1)}, s32[]{:S(2)}) async-start(s8[4718592]{0:T(1024)(128)(4,1)} %bitcast.90), calls=%async_computation.4 | async-start | bytes 1048576
  510.7 55.9 %slice-start.1 = ((s8[4718592]{0:T(1024)(128)(4,1)}), s8[4194304]{0:T(1024)(128)(4,1)S(1)}, s32[]{:S(2)}) async-start(s8[4718592]{0:T(1024)(128)(4,1)} %bitcast.90), calls=%async_computation.5 | async-start | bytes 8388608
  566.6 369.2 %copy-start.1 = (bf16[1,128,1920]{2,1,0:T(8,128)(2,1)S(1)}, bf16[1,128,1920]{2,1,0:T(8,128)(2,1)}, u32[]{:S(2)}) copy-start(bf16[1,128,1920]{2,1,0:T(8,128)(2,1)} %param.10) | copy-start | bytes 1474564
Sparse Core Ops, SparseCore 0:
  9.8 97.2 all-gather.1
  109.6 381.1 reduce-scatter.1
  493.5 440.9 all-reduce.2
where the time goes:
time: 944 us; the launch traced here: 942 us
  waiting for transfers between devices  765 us (81%)
  starting transfers between devices  67.6 us (7%)
  matrix products  51.1 us (5%)
  local copies, waits for them, and re-layouts  27 us (3%)
  other arithmetic  16.6 us (2%)
  between operations  14.8 us (2%)
    unnamed x4, waiting for transfers between devices  363 us
    reduce_scatter x1, waiting for transfers between devices, per_device(): lax.psum_scatter(lax.dot_general(attn, grad_rows, (((0,), (0,)), ((), ())...  332 us
    ppermute x16, starting transfers between devices, from_behind(): lax.ppermute(value, axis, [(source, source + steps) for source in range(l...  67.3 us
    ppermute x16, waiting for transfers between devices, from_behind(): lax.ppermute(value, axis, [(source, source + steps) for source in range(l...  63.8 us
  transfers between devices with their start and end apart: 19, of which 10 were waited for; matrix products, arithmetic and copies ran while one was open for 10% of the time, Pallas kernels for 0%

commit v1 on v0

v1 whole, which is shorter than its diff:
```python
import functools

import jax
import jax.numpy as jnp
from jax import lax
from jax.experimental import pallas as pl
from jax.experimental.pallas import tpu as pltpu
from jax.sharding import PartitionSpec as P

HEAD = 256
BLOCK = 128
WINDOW = 1024
SLOTS = 9
ROWS = SLOTS * BLOCK
MESH = pl.DeviceIdType.MESH
F32 = jnp.float32
BF16 = jnp.bfloat16


def device_at(x, y, z, core):
    return (lax.rem(z, 2) * 4 + x, (lax.div(z, 2) * 4 + y) * 2 + core)


def dot(a, b, ca, cb):
    return lax.dot_general(a, b, (((ca,), (cb,)), ((), ())), preferred_element_type=F32)


def kernel(
    normaliser,
    doc_ref, q_ref, k_ref, v_ref, w_ref, og_ref,
    lo_ref, dq_ref, dk_ref, dv_ref, wg_ref,
    own_st, zbuf, win, qh, og_all, w_all, ga_st, ga, bias, shares, attn_loc, attn_all,
    dq_st, dq_rx, dkv, d0_rx, d4_rx, dy_rx, acc, rel_st, dz_rx,
    wg_st, wy_rx, wsum, wz_rx, lp_st, lp_rx, lo_own, lx_st, lx_rx,
    q_sem, og_s, og_r, ogp_s, ogp_r, w_s, w_r, zk_s, zk_r, yk_s, yk_r, pk_s, pk_r, p0_s, p0_r,
    ga_s, ga_r, at_s, at_r, dqs, dqr, d0s, d0r, d4s, d4r, yd_s, yd_r, zd_s, zd_r,
    wy_s, wy_r, wz_s, wz_r, lp_s, lp_r, lx_s, lx_r,
):
    dp = lax.axis_index("dp")
    s = lax.axis_index("seq")
    x, zl = lax.rem(dp, 4), lax.div(dp, 4)
    q, y, zh = lax.rem(s, 2), lax.rem(lax.div(s, 2), 4), lax.div(s, 8)
    z = zh * 2 + zl
    other = 1 - q
    partner = device_at(x, y, z, other)
    scale = HEAD ** (-0.5)

    def mine(i):
        return pl.ds(pl.multiple_of(i * BLOCK, BLOCK), BLOCK)

    def remote(src, dst, ss, rs, dev):
        return pltpu.make_async_remote_copy(
            src_ref=src, dst_ref=dst, send_sem=ss, recv_sem=rs, device_id=dev, device_id_type=MESH
        )

    xs = [lax.rem(x + k, 4) for k in range(4)]
    ys = [lax.rem(y + k, 4) for k in range(4)]

    barrier = pltpu.get_barrier_semaphore()
    count = 0
    for k in range(1, 4):
        pl.semaphore_signal(barrier, 1, device_id=device_at(xs[k], y, z, q), device_id_type=MESH)
        for core in range(2):
            pl.semaphore_signal(
                barrier, 1, device_id=device_at(x, ys[k], z, core), device_id_type=MESH
            )
        count += 3
    pl.semaphore_signal(barrier, 1, device_id=partner, device_id_type=MESH)
    count += 1
    for k in range(1, 8):
        for core in range(2):
            pl.semaphore_signal(
                barrier, 1, device_id=device_at(x, y, lax.rem(z + k, 8), core), device_id_type=MESH
            )
        count += 2

    for half in range(2):
        own_st[half, :, 0:512] = k_ref[:, half * 512 : half * 512 + 512]
        own_st[half, :, 512:1024] = v_ref[:, half * 512 : half * 512 + 512]
    pl.semaphore_wait(barrier, count)

    sends = []

    def go(copy):
        copy.start()
        sends.append(copy)
        return copy

    for half in range(2):
        go(remote(own_st.at[half], zbuf.at[half], zk_s.at[half], zk_r.at[half],
                  device_at(x, y, lax.rem(z + 2, 8), q)))

    def along_y(k, half, src):
        return remote(
            src.at[half], win.at[mine(7 - 2 * k + q)], yk_s.at[k - 1, half], yk_r.at[k - 1, q],
            device_at(x, ys[k], z, half),
        )

    for k in range(1, 4):
        @pl.when(y + k < 4)
        def _():
            for half in range(2):
                along_y(k, half, own_st).start()

    og_cp = {}
    for k in (1, 3, 2):
        og_cp[k] = go(remote(og_ref, og_all.at[4 - k, mine(q)], og_s.at[k], og_r.at[4 - k],
                             device_at(xs[k], y, z, q)))
    go(remote(w_ref.at[mine(q)], w_all.at[mine(q)], w_s, w_r.at[q],
              device_at(x, y, lax.rem(z + 9 - 2 * q, 8), zl)))
    go(remote(own_st.at[other], win.at[mine(7 + q)], pk_s, pk_r, partner))
    go(remote(q_ref.at[:, pl.ds(pl.multiple_of(other * 1024, 1024), 1024)], qh.at[mine(q)],
              q_sem.at[0], q_sem.at[1], partner))
    go(remote(og_ref, og_all.at[0, mine(q)], ogp_s.at[0], ogp_r.at[0], partner))

    win[mine(7 + q), :] = own_st[q]
    qh[mine(q), :] = q_ref[:, pl.ds(pl.multiple_of(q * 1024, 1024), 1024)]
    og_all[0, mine(q), :] = og_ref[...]

    chip = zh * 4 + y
    qp = chip * 256 + lax.broadcasted_iota(jnp.int32, (256, 1), 0)
    kp = (chip * 2 - 7) * BLOCK + lax.broadcasted_iota(jnp.int32, (1, ROWS), 1)
    qd = jnp.zeros((256, 1), jnp.int32)
    kd = jnp.zeros((1, ROWS), jnp.int32)
    start = jnp.int32(0)
    for n in range(8):
        qd = qd + (start <= qp).astype(jnp.int32)
        kd = kd + (start <= kp).astype(jnp.int32)
        start = start + doc_ref[0, n] * BLOCK
    allowed = (kp <= qp) & (kp > qp - WINDOW) & (kd == qd)
    bias[...] = jnp.where(allowed, 0.0, -jnp.inf).astype(F32)

    @pl.when(q == zl)
    def _():
        w_all[...] = w_ref[...]

    def relay(half):
        remote(own_st.at[half], zbuf.at[half], zk_s.at[half], zk_r.at[half], partner).wait_recv()
        for k in range(1, 4):
            @pl.when(y + k >= 4)
            def _():
                along_y(k, half, zbuf).start()

    def og_forward(r):
        og_cp[4 - r].wait_recv()
        go(remote(og_all.at[r, mine(q)], og_all.at[r, mine(q)], ogp_s.at[r], ogp_r.at[r], partner))

    relay(0)
    for r in (1, 3, 2):
        og_forward(r)

    @pl.when(q != zl)
    def _():
        for j in range(2):
            remote(w_ref.at[pl.ds(0, BLOCK)], w_all.at[pl.ds(j * BLOCK, BLOCK)], w_s, w_r.at[j],
                   partner).wait_recv()

    ga_cp = []
    for r in (1, 3, 2, 0):
        remote(og_ref, og_all.at[r, mine(other)], ogp_s.at[r], ogp_r.at[r], partner).wait_recv()
        part = dot(og_all[r], w_all[...], 1, 1).astype(BF16)
        if r == 0:
            ga[x] = part
        else:
            ga_st[r - 1] = part
            ga_cp.append(go(remote(ga_st.at[r - 1], ga.at[x], ga_s.at[r - 1], ga_r.at[r - 1],
                                   device_at(xs[r], y, z, q))))
    relay(1)

    @pl.when(q == 1)
    def _():
        remote(zbuf.at[0], win.at[pl.ds(0, BLOCK)], p0_s, p0_r, partner).start()
        win[0:BLOCK, :] = zbuf[1]

    remote(own_st.at[0], win.at[mine(7 + other)], pk_s, pk_r, partner).wait_recv()
    remote(q_ref.at[:, pl.ds(0, 1024)], qh.at[mine(other)], q_sem.at[0], q_sem.at[1],
           partner).wait_recv()
    for k in range(1, 4):
        for j in range(2):
            remote(own_st.at[0], win.at[mine(7 - 2 * k + j)], yk_s.at[k - 1, 0], yk_r.at[k - 1, j],
                   partner).wait_recv()

    @pl.when(q == 0)
    def _():
        remote(zbuf.at[0], win.at[pl.ds(0, BLOCK)], p0_s, p0_r, partner).wait_recv()

    def lanes(i):
        return pl.ds(pl.multiple_of(i * HEAD, HEAD), HEAD)

    def forward(h, carry):
        m = lax.div(h, 2)
        scores = dot(qh[:, lanes(h)], win[:, lanes(m)], 1, 1) * scale + bias[...]
        top = jnp.max(scores, axis=-1, keepdims=True)
        lifted = jnp.exp(scores - top)
        share = lifted * (1.0 / jnp.sum(lifted, axis=-1, keepdims=True))
        shares[h] = share
        attn_loc[h] = dot(share.astype(BF16), win[:, lanes(m + 2)], 1, 0).astype(BF16)
        return carry

    lax.fori_loop(0, 4, forward, 0)

    at_cp = []
    for k in (1, 3, 2):
        at_cp.append(go(remote(attn_loc.at[xs[k]], attn_all.at[4 - k], at_s.at[k - 1],
                               at_r.at[k - 1], device_at(xs[k], y, z, q))))
    attn_all[0] = attn_loc[x]

    for copy in ga_cp:
        copy.wait_recv()

    def backward(m, carry):
        dk = jnp.zeros((ROWS, HEAD), F32)
        dv = jnp.zeros((ROWS, HEAD), F32)
        for g in range(2):
            h = m * 2 + g
            share = shares[h]
            gh = ga[h]
            gs = dot(gh, win[:, lanes(m + 2)], 1, 1)
            centre = jnp.sum(share * gs, axis=-1, keepdims=True)
            ds = (share * (gs - centre) * scale).astype(BF16)
            dq_st[h] = dot(ds, win[:, lanes(m)], 1, 0).astype(BF16)
            dk = dk + dot(ds, qh[:, lanes(h)], 0, 0)
            dv = dv + dot(share.astype(BF16), gh, 0, 0)
        dkv[:, lanes(m)] = dk.astype(BF16)
        dkv[:, lanes(m + 2)] = dv.astype(BF16)
        return carry

    lax.fori_loop(0, 2, backward, 0)

    yd_cp = {}
    for k in (3, 2, 1):
        for j in range(2):
            yd_cp[k, j] = go(remote(
                dkv.at[pl.ds((7 - 2 * k + j) * BLOCK, BLOCK)], dy_rx.at[k - 1, q],
                yd_s.at[k - 1, j], yd_r.at[k - 1, q], device_at(x, ys[4 - k], z, j)))

    @pl.when(q == 0)
    def _():
        remote(dkv.at[pl.ds(0, BLOCK)], d4_rx, d4s, d4r, partner).start()

    go(remote(dkv.at[mine(7 + other)], d0_rx, d0s, d0r, partner))
    go(remote(dq_st.at[:, mine(other)], dq_rx, dqs, dqr, partner))

    for copy in at_cp:
        copy.wait_recv()
    lp_cp = []
    for r in (1, 3, 2, 0):
        lp_st[r] = dot(attn_all[r, mine(other), :], w_all[...], 1, 0).astype(BF16)
        lp_cp.append(go(remote(lp_st.at[r], lp_rx.at[r], lp_s.at[r], lp_r.at[r], partner)))
        lo_own[r] = dot(attn_all[r, mine(q), :], w_all[...], 1, 0)

    acc[...] = jnp.zeros_like(acc)

    def dy_wait(k):
        for half in range(2):
            remote(own_st.at[0], dy_rx.at[k - 1, half], yd_s.at[0, 0], yd_r.at[k - 1, half],
                   partner).wait_recv()

    @pl.when(q == 1)
    def _():
        remote(own_st.at[0], d4_rx, d4s, d4r, partner).wait_recv()
        acc[0] = d4_rx[...].astype(F32)
        acc[1] = dkv[0:BLOCK, :].astype(F32)

    for k in (3, 2, 1):
        @pl.when(y + k >= 4)
        def _():
            dy_wait(k)
            acc[...] += dy_rx[k - 1].astype(F32)
    for half in range(2):
        rel_st[half] = acc[half].astype(BF16)
        go(remote(rel_st.at[half], dz_rx.at[half], zd_s.at[half], zd_r.at[half],
                  device_at(x, y, lax.rem(z + 6, 8), q)))

    lx_cp = []
    for i, r in enumerate((1, 3, 2)):
        lp_cp[i].wait_recv()
        lx_st[r - 1] = (lo_own[r] + lp_rx[r].astype(F32)).astype(BF16)
        lx_cp.append(go(remote(lx_st.at[r - 1], lx_rx.at[r - 1], lx_s.at[r - 1], lx_r.at[r - 1],
                               device_at(xs[r], y, z, q))))
    lp_cp[3].wait_recv()

    product = dot(attn_all[...].reshape(1024, HEAD), og_all[...].reshape(1024, og_ref.shape[1]), 0, 0)
    for yy in range(4):
        for zz in range(4):
            wg_st[yy, zz * 16 : zz * 16 + 16, :] = product[
                (zz * 4 + yy) * 16 : (zz * 4 + yy) * 16 + 16, :
            ].astype(BF16)
    wy_cp = []
    for k in (1, 3, 2):
        wy_cp.append(go(remote(wg_st.at[ys[k]], wy_rx.at[k - 1], wy_s.at[k - 1], wy_r.at[k - 1],
                               device_at(x, ys[k], z, q))))

    dq_mine = dq_st[:, mine(q), :]
    remote(dq_rx, dq_rx, dqs, dqr, partner).wait_recv()
    for h in range(4):
        dq_ref[:, lanes(q * 4 + h)] = dq_mine[h]
        dq_ref[:, lanes(other * 4 + h)] = dq_rx[h]

    for copy in wy_cp:
        copy.wait_recv()
    total = wg_st[y].astype(F32)
    for k in range(3):
        total = total + wy_rx[k].astype(F32)
    wsum[...] = total.reshape(8, 8, total.shape[-1])

    def to_z(i):
        return remote(wsum.at[i], wz_rx.at[z], wz_s.at[i], wz_r.at[z],
                      device_at(x, y, (i // 2) * 2 + q, i % 2))

    for i in range(8):
        here = ((i // 2) * 2 + q == z) & (q == i % 2)

        @pl.when(jnp.logical_not(here))
        def _():
            to_z(i).start()

        @pl.when(here)
        def _():
            wz_rx[z] = wsum[i]

    out = lo_own[0] + lp_rx[0].astype(F32)
    for i, r in enumerate((1, 3, 2)):
        lx_cp[i].wait_recv()
        out = out + lx_rx[r - 1].astype(F32)
    lo_ref[...] = out.astype(BF16)

    remote(own_st.at[0], d0_rx, d0s, d0r, partner).wait_recv()
    acc[q] = dkv[mine(7 + q), :].astype(F32)
    acc[other] = d0_rx[...].astype(F32)
    for k in (3, 2, 1):
        @pl.when(y + k < 4)
        def _():
            dy_wait(k)
            acc[...] += dy_rx[k - 1].astype(F32)
    for half in range(2):
        remote(rel_st.at[half], dz_rx.at[half], zd_s.at[half], zd_r.at[half], partner).wait_recv()
        own = (acc[half] + dz_rx[half].astype(F32)).astype(BF16)
        dk_ref[:, half * 512 : half * 512 + 512] = own[:, 0:512]
        dv_ref[:, half * 512 : half * 512 + 512] = own[:, 512:1024]

    for src in range(8):
        here = (z == src) & (zl == q)

        @pl.when(jnp.logical_not(here))
        def _():
            remote(wsum.at[0], wz_rx.at[src], wz_s.at[0], wz_r.at[src], partner).wait_recv()

    wg_ref[...] = jnp.sum(wz_rx[...], axis=0) * normaliser

    for copy in sends:
        copy.wait_send()
    for k in range(1, 4):
        for half in range(2):
            along_y(k, half, own_st).wait_send()
    for i in range(8):
        here = ((i // 2) * 2 + q == z) & (q == i % 2)

        @pl.when(jnp.logical_not(here))
        def _():
            to_z(i).wait_send()

    @pl.when(q == 1)
    def _():
        remote(zbuf.at[0], win.at[pl.ds(0, BLOCK)], p0_s, p0_r, partner).wait_send()

    @pl.when(q == 0)
    def _():
        remote(dkv.at[pl.ds(0, BLOCK)], d4_rx, d4s, d4r, partner).wait_send()


def per_device(query, keys, values, out_weight, out_grad, doc_blocks):
    width = out_grad.shape[2]
    tokens = lax.axis_size("dp") * lax.axis_size("seq") * BLOCK
    vmem = pl.BlockSpec(memory_space=pltpu.VMEM)
    dma = pltpu.SemaphoreType.DMA
    scratch = [
        ((2, BLOCK, 1024), BF16),
        ((2, BLOCK, 1024), BF16),
        ((ROWS, 1024), BF16),
        ((256, 1024), BF16),
        ((4, 256, width), BF16),
        ((HEAD, width), BF16),
        ((3, 256, HEAD), BF16),
        ((4, 256, HEAD), BF16),
        ((256, ROWS), F32),
        ((4, 256, ROWS), F32),
        ((4, 256, HEAD), BF16),
        ((4, 256, HEAD), BF16),
        ((4, 256, HEAD), BF16),
        ((4, BLOCK, HEAD), BF16),
        ((ROWS, 1024), BF16),
        ((BLOCK, 1024), BF16),
        ((BLOCK, 1024), BF16),
        ((3, 2, BLOCK, 1024), BF16),
        ((2, BLOCK, 1024), F32),
        ((2, BLOCK, 1024), BF16),
        ((2, BLOCK, 1024), BF16),
        ((4, 64, width), BF16),
        ((3, 64, width), BF16),
        ((8, 8, width), F32),
        ((8, 8, width), F32),
        ((4, BLOCK, width), BF16),
        ((4, BLOCK, width), BF16),
        ((4, BLOCK, width), F32),
        ((3, BLOCK, width), BF16),
        ((3, BLOCK, width), BF16),
    ]
    semaphores = [
        (2,), (4,), (4,), (4,), (4,), (), (2,), (2,), (2,), (3, 2), (3, 2), (), (), (), (),
        (3,), (3,), (3,), (3,), (), (), (), (), (), (), (3, 2), (3, 2), (2,), (2,),
        (3,), (3,), (8,), (8,), (4,), (4,), (3,), (3,),
    ]
    layer_out, query_grad, key_gradient, value_gradient, weight_grad = pl.pallas_call(
        functools.partial(kernel, tokens ** (-0.5)),
        out_shape=[
            jax.ShapeDtypeStruct((BLOCK, width), BF16),
            jax.ShapeDtypeStruct((BLOCK, 2048), BF16),
            jax.ShapeDtypeStruct((BLOCK, 1024), BF16),
            jax.ShapeDtypeStruct((BLOCK, 1024), BF16),
            jax.ShapeDtypeStruct((8, width), F32),
        ],
        in_specs=[pl.BlockSpec(memory_space=pltpu.SMEM)] + [vmem] * 5,
        out_specs=[vmem] * 5,
        scratch_shapes=[pltpu.VMEM(*a) for a in scratch]
        + [dma(a) if a else dma for a in semaphores],
        compiler_params=pltpu.CompilerParams(
            collective_id=0, has_side_effects=True, vmem_limit_bytes=60 << 20
        ),
    )(doc_blocks, query[0], keys[0], values[0], out_weight, out_grad[0])
    return (
        layer_out[None],
        query_grad[None],
        key_gradient[None],
        value_gradient[None],
        weight_grad,
    )


def solution(mesh):
    tokens = P("dp", "seq", None)
    return jax.shard_map(
        per_device,
        mesh=mesh,
        in_specs=(tokens, tokens, tokens, P("dp", None), tokens, P("dp", None)),
        out_specs=(tokens, tokens, tokens, tokens, P(("dp", "seq"), None)),
        check_vma=False,
    )
```

time: 944 us -> 122 us (0.13)
  the two profiles are of different devices: /device:TPU:1 before, /device:TPU:53 now
where the time goes in v1:
time: 122 us; the launch traced here: 121 us
  Pallas kernels  115 us (94%)
  local copies, waits for them, and re-layouts  5.52 us (5%)
    pallas_call x1, Pallas kernels, per_device(): pl.pallas_call(functools.partial(kernel, tokens ** (-0.5)), out_shape=[ja...  115 us
    unnamed x13, local copies, waits for them, and re-layouts  5.52 us

profile of v1, /device:TPU:53, one launch (start us, length us, event | category | flops | bytes accessed | tf_op | source)
XLA Modules:
  0.0 121.3 jit_solution(16983954467398590650)
XLA Ops:
  0.6 115.1 %shard_map.101 = (bf16[128,1920]{1,0:T(8,128)(2,1)}, bf16[128,2048]{1,0:T(8,128)(2,1)}, bf16[128,1024]{1,0:T(8,128)(2,1)}, bf16[128,1024]{1,0:T(8,128)(2,1)}, f32[8,1920]{1,0:T(8,128)}) custom-call(s32[1,8]{1,0:T(1,128)} %doc_ref.1, bf16[128,2048]{1,0:T(8,128)(2,1)} %bitcast.9, bf16[128,1024]{1,0:T(8,128)(2,1)} %bitcast.14, bf16[128,1024]{1,0:T(8,128)(2,1)} %bitcast.15, ...), custom_call_target="tpu_custom_call" | custom-call | tf_op jit(solution)/shard_map/pallas_call | solution.py:414
  115.7 0.0 copy-start
  115.7 1.9 %copy.16 = bf16[1,128,1920]{2,1,0:T(8,128)(2,1)} copy(bf16[1,128,1920]{2,1,0:T(8,128)(2,1)} %bitcast.11) | data formatting | bytes 983040
  117.6 0.0 copy-done
  117.7 0.0 copy-start.2
  117.7 0.8 copy.17
  118.4 0.3 copy-done.2
  118.7 0.0 copy-start.1
  118.7 0.7 copy.18
  119.4 0.3 copy-done.1
  119.8 0.0 copy-start.3
  119.8 0.7 copy.19
  120.5 0.1 copy-done.3
  120.6 0.6 copy.20
Async XLA Ops:
  115.7 1.9 %copy-start = (bf16[128,2048]{1,0:T(8,128)(2,1)S(1)}, bf16[128,2048]{1,0:T(8,128)(2,1)}, u32[]{:S(2)}) copy-start(bf16[128,2048]{1,0:T(8,128)(2,1)} %get-tuple-element.11) | copy-start | bytes 1572868
  117.7 1.1 copy-start.2
  118.7 1.0 copy-start.1
  119.8 0.9 copy-start.3

commit v2 on v1

v2 whole, which is shorter than its diff:
```python
import functools

import jax
import jax.numpy as jnp
from jax import lax
from jax.experimental import pallas as pl
from jax.experimental.pallas import tpu as pltpu
from jax.sharding import PartitionSpec as P

HEAD = 256
BLOCK = 128
WINDOW = 1024
SLOTS = 9
ROWS = SLOTS * BLOCK
SPLIT = 1152
MESH = pl.DeviceIdType.MESH
F32 = jnp.float32
BF16 = jnp.bfloat16


def device_at(x, y, z, core):
    return (lax.rem(z, 2) * 4 + x, (lax.div(z, 2) * 4 + y) * 2 + core)


def dot(a, b, ca, cb):
    return lax.dot_general(a, b, (((ca,), (cb,)), ((), ())), preferred_element_type=F32)


def kernel(
    normaliser,
    doc_ref, q_ref, k_ref, v_ref, w_ref, og_ref,
    lo_ref, dq_ref, dk_ref, dv_ref, wg_ref,
    own_st, zbuf, win, qh, og_all, w_all, ga_st, ga, bias, shares, attn_loc, attn_all,
    dq_st, dq_rx, dkv, d0_rx, d4_rx, dy_rx, acc, rel_st, dz_rx,
    wg_st, wy_rx, wsum, wz_rx, wp_st, wp_rx, lp_st, lp_rx, lo_own, lx_st, lx_rx, wx, lt_st, lt_rx, lt_own,
    q_sem, og_s, og_r, ogp_s, ogp_r, w_s, w_r, zk_s, zk_r, yk_s, yk_r, pk_s, pk_r, p0_s, p0_r,
    ga_s, ga_r, at_s, at_r, dqs, dqr, d0s, d0r, d4s, d4r, yd_s, yd_r, zd_s, zd_r,
    wy_s, wy_r, wz_s, wz_r, wp_s, wp_r, lp_s, lp_r, lx_s, lx_r,
    wx_s, wx_r, lt_s, lt_r,
):
    dp = lax.axis_index("dp")
    s = lax.axis_index("seq")
    x, zl = lax.rem(dp, 4), lax.div(dp, 4)
    q, y, zh = lax.rem(s, 2), lax.rem(lax.div(s, 2), 4), lax.div(s, 8)
    z = zh * 2 + zl
    other = 1 - q
    partner = device_at(x, y, z, other)
    scale = HEAD ** (-0.5)
    split = SPLIT

    def mine(i):
        return pl.ds(pl.multiple_of(i * BLOCK, BLOCK), BLOCK)

    def remote(src, dst, ss, rs, dev):
        return pltpu.make_async_remote_copy(
            src_ref=src, dst_ref=dst, send_sem=ss, recv_sem=rs, device_id=dev, device_id_type=MESH
        )

    xs = [lax.rem(x + k, 4) for k in range(4)]
    ys = [lax.rem(y + k, 4) for k in range(4)]

    barrier = pltpu.get_barrier_semaphore()
    count = 0
    for k in range(1, 4):
        pl.semaphore_signal(barrier, 1, device_id=device_at(xs[k], y, z, q), device_id_type=MESH)
        for core in range(2):
            pl.semaphore_signal(
                barrier, 1, device_id=device_at(x, ys[k], z, core), device_id_type=MESH
            )
        count += 3
    pl.semaphore_signal(barrier, 1, device_id=partner, device_id_type=MESH)
    count += 1
    for k in range(1, 8):
        for core in range(2):
            pl.semaphore_signal(
                barrier, 1, device_id=device_at(x, y, lax.rem(z + k, 8), core), device_id_type=MESH
            )
        count += 2

    for half in range(2):
        for m in range(2):
            lo = half * 512 + m * HEAD
            own_st[m, half, :, 0:HEAD] = k_ref[:, lo : lo + HEAD]
            own_st[m, half, :, HEAD : 2 * HEAD] = v_ref[:, lo : lo + HEAD]
    pl.semaphore_wait(barrier, count)

    sends = []

    def go(copy):
        copy.start()
        sends.append(copy)
        return copy

    def up_z(m):
        return remote(own_st.at[m], zbuf.at[m], zk_s.at[m], zk_r.at[m],
                      device_at(x, y, lax.rem(z + 2, 8), q))

    def along_y(m, k, half, src):
        return remote(
            src.at[m, half], win.at[m, mine(7 - 2 * k + q)], yk_s.at[m, k - 1, half],
            yk_r.at[m, k - 1, q], device_at(x, ys[k], z, half),
        )

    def og_send(k):
        return go(remote(og_ref, og_all.at[4 - k, mine(q)], og_s.at[k], og_r.at[4 - k],
                         device_at(xs[k], y, z, q)))

    up_z(0).start()
    up_z(1).start()
    og_cp = {1: og_send(1), 3: og_send(3)}
    for m in range(2):
        for k in range(1, 4):
            @pl.when(y + k < 4)
            def _():
                for half in range(2):
                    along_y(m, k, half, own_st).start()

    go(remote(w_ref.at[mine(q)], w_all.at[mine(q)], w_s, w_r.at[q],
              device_at(x, y, lax.rem(z + 7, 8), zl)))
    go(remote(og_ref, og_all.at[0, mine(q)], ogp_s.at[0], ogp_r.at[0], partner))
    for m in range(2):
        go(remote(own_st.at[m, other], win.at[m, mine(7 + q)], pk_s.at[m], pk_r.at[m], partner))
    go(remote(q_ref.at[:, pl.ds(pl.multiple_of(other * 1024, 1024), 1024)], qh.at[mine(q)],
              q_sem.at[0], q_sem.at[1], partner))

    for m in range(2):
        win[m, mine(7 + q), :] = own_st[m, q]
    qh[mine(q), :] = q_ref[:, pl.ds(pl.multiple_of(q * 1024, 1024), 1024)]
    og_all[0, mine(q), :] = og_ref[...]

    chip = zh * 4 + y
    qp = chip * 256 + lax.broadcasted_iota(jnp.int32, (256, 1), 0)
    kp = (chip * 2 - 7) * BLOCK + lax.broadcasted_iota(jnp.int32, (1, ROWS), 1)
    qd = jnp.zeros((256, 1), jnp.int32)
    kd = jnp.zeros((1, ROWS), jnp.int32)
    start = jnp.int32(0)
    for n in range(8):
        qd = qd + (start <= qp).astype(jnp.int32)
        kd = kd + (start <= kp).astype(jnp.int32)
        start = start + doc_ref[0, n] * BLOCK
    allowed = (kp <= qp) & (kp > qp - WINDOW) & (kd == qd)
    bias[...] = jnp.where(allowed, 0.0, -jnp.inf).astype(F32)

    @pl.when(q == zl)
    def _():
        w_all[...] = w_ref[...]

    def relay(m):
        up_z(m).wait_recv()
        for k in range(1, 4):
            @pl.when(y + k >= 4)
            def _():
                for half in range(2):
                    along_y(m, k, half, zbuf).start()

        @pl.when(q == 1)
        def _():
            remote(zbuf.at[m, 0], win.at[m, pl.ds(0, BLOCK)], p0_s.at[m], p0_r.at[m],
                   partner).start()
            win[m, 0:BLOCK, :] = zbuf[m, 1]

    def og_forward(r):
        og_cp[4 - r].wait_recv()
        go(remote(og_all.at[r, mine(q)], og_all.at[r, mine(q)], ogp_s.at[r], ogp_r.at[r], partner))

    def head_gradient(r):
        remote(og_ref, og_all.at[r, mine(other)], ogp_s.at[r], ogp_r.at[r], partner).wait_recv()
        part = dot(og_all[r], w_all[...], 1, 1).astype(BF16)
        if r == 0:
            ga[x] = part
        else:
            ga_st[r - 1] = part
            go(remote(ga_st.at[r - 1], ga.at[x], ga_s.at[r - 1], ga_r.at[x],
                      device_at(xs[r], y, z, q)))

    def window_wait(m):
        remote(own_st.at[0, 0], win.at[m, mine(7 + other)], pk_s.at[m], pk_r.at[m],
               partner).wait_recv()
        for k in range(1, 4):
            for j in range(2):
                remote(own_st.at[0, 0], win.at[m, mine(7 - 2 * k + j)], yk_s.at[m, 0, 0],
                       yk_r.at[m, k - 1, j], partner).wait_recv()

        @pl.when(q == 0)
        def _():
            remote(zbuf.at[m, 0], win.at[m, pl.ds(0, BLOCK)], p0_s.at[m], p0_r.at[m],
                   partner).wait_recv()

    def lanes(i):
        return pl.ds(pl.multiple_of(i * HEAD, HEAD), HEAD)

    def attn_copy(h):
        r = lax.rem(x - h + 4, 4)
        return remote(attn_loc.at[h], attn_all.at[r], at_s.at[h], at_r.at[r],
                      device_at(jnp.int32(h), y, z, q))

    def forward(m):
        for g in range(2):
            h = m * 2 + g
            scores = dot(qh[:, h * HEAD : h * HEAD + HEAD], win[m, :, 0:HEAD], 1, 1) * scale
            scores = scores + bias[...]
            top = jnp.max(scores, axis=-1, keepdims=True)
            lifted = jnp.exp(scores - top)
            share = lifted * (1.0 / jnp.sum(lifted, axis=-1, keepdims=True))
            shares[g] = share
            attn_loc[h] = dot(share.astype(BF16), win[m, :, HEAD:], 1, 0).astype(BF16)

            @pl.when(x != h)
            def _():
                attn_copy(h).start()

            @pl.when(x == h)
            def _():
                attn_all[0] = attn_loc[h]

    def dy_copy(m, k, j):
        return remote(
            dkv.at[m, pl.ds((7 - 2 * k + j) * BLOCK, BLOCK)], dy_rx.at[m, k - 1, q],
            yd_s.at[m, k - 1, j], yd_r.at[m, k - 1, q], device_at(x, ys[4 - k], z, j))

    def backward(m):
        dk = jnp.zeros((ROWS, HEAD), F32)
        dv = jnp.zeros((ROWS, HEAD), F32)
        for g in range(2):
            h = m * 2 + g

            @pl.when(x != h)
            def _():
                remote(ga_st.at[0], ga.at[h], ga_s.at[0], ga_r.at[h], partner).wait_recv()

            share = shares[g]
            gh = ga[h]
            gs = dot(gh, win[m, :, HEAD:], 1, 1)
            centre = jnp.sum(share * gs, axis=-1, keepdims=True)
            ds = (share * (gs - centre) * scale).astype(BF16)
            dq_st[h] = dot(ds, win[m, :, 0:HEAD], 1, 0).astype(BF16)
            dk = dk + dot(ds, qh[:, h * HEAD : h * HEAD + HEAD], 0, 0)
            dv = dv + dot(share.astype(BF16), gh, 0, 0)
        dkv[m, :, 0:HEAD] = dk.astype(BF16)
        dkv[m, :, HEAD:] = dv.astype(BF16)

        for k in (3, 2, 1):
            for j in range(2):
                go(dy_copy(m, k, j))

        @pl.when(q == 0)
        def _():
            remote(dkv.at[m, pl.ds(0, BLOCK)], d4_rx.at[m], d4s.at[m], d4r.at[m], partner).start()

        go(remote(dkv.at[m, mine(7 + other)], d0_rx.at[m], d0s.at[m], d0r.at[m], partner))

    def dy_add(m, k):
        for half in range(2):
            remote(own_st.at[0, 0], dy_rx.at[m, k - 1, half], yd_s.at[0, 0, 0],
                   yd_r.at[m, k - 1, half], partner).wait_recv()
        acc[m] += dy_rx[m, k - 1].astype(F32)

    def down_z(m):
        return remote(rel_st.at[m], dz_rx.at[m], zd_s.at[m], zd_r.at[m],
                      device_at(x, y, lax.rem(z + 6, 8), q))

    def relay_sums(m):
        acc[m] = jnp.zeros_like(acc[m])

        @pl.when(q == 1)
        def _():
            remote(own_st.at[0, 0], d4_rx.at[m], d4s.at[m], d4r.at[m], partner).wait_recv()
            acc[m, 0] = d4_rx[m].astype(F32)
            acc[m, 1] = dkv[m, 0:BLOCK, :].astype(F32)

        for k in (3, 2, 1):
            @pl.when(y + k >= 4)
            def _():
                dy_add(m, k)
        rel_st[m] = acc[m].astype(BF16)
        go(down_z(m))

    def own_sums(m):
        remote(own_st.at[0, 0], d0_rx.at[m], d0s.at[m], d0r.at[m], partner).wait_recv()
        acc[m, q] = dkv[m, mine(7 + q), :].astype(F32)
        acc[m, other] = d0_rx[m].astype(F32)
        for k in (3, 2, 1):
            @pl.when(y + k < 4)
            def _():
                dy_add(m, k)

    def own_finish(m):
        down_z(m).wait_recv()
        for half in range(2):
            own = (acc[m, half] + dz_rx[m, half].astype(F32)).astype(BF16)
            lo = half * 512 + m * HEAD
            dk_ref[:, lo : lo + HEAD] = own[:, 0:HEAD]
            dv_ref[:, lo : lo + HEAD] = own[:, HEAD:]

    def weight_wait():
        @pl.when(q != zl)
        def _():
            for j in range(2):
                remote(w_ref.at[pl.ds(0, BLOCK)], w_all.at[pl.ds(j * BLOCK, BLOCK)], w_s,
                       w_r.at[j], partner).wait_recv()

    def query_wait():
        remote(q_ref.at[:, pl.ds(0, 1024)], qh.at[mine(other)], q_sem.at[0], q_sem.at[1],
               partner).wait_recv()

    def attn_wait():
        for r in (1, 3, 2):
            remote(attn_loc.at[0], attn_all.at[r], at_s.at[0], at_r.at[r], partner).wait_recv()

    def wx_copy(k):
        return remote(w_all.at[:, split:], wx.at[x], wx_s.at[k - 1], wx_r.at[x],
                      device_at(xs[k], y, z, q))

    def wx_send():
        wx[x] = w_all[:, split:]
        for k in (1, 3, 2):
            go(wx_copy(k))

    def tail_copy():
        return remote(lt_st, lt_rx, lt_s, lt_r, partner)

    def tail_product():
        for h in range(4):
            @pl.when(x != h)
            def _():
                remote(wx.at[0], wx.at[h], wx_s.at[0], wx_r.at[h], partner).wait_recv()

        lt_st[...] = sum(dot(attn_loc[h, mine(other), :], wx[h], 1, 0) for h in range(4))
        go(tail_copy())
        lt_own[...] = sum(dot(attn_loc[h, mine(q), :], wx[h], 1, 0) for h in range(4))

    def tail_finish():
        tail_copy().wait_recv()
        lo_ref[:, split:] = (lt_own[...] + lt_rx[...]).astype(BF16)

    def lo_pair(r):
        return remote(lp_st.at[r], lp_rx.at[r], lp_s.at[r], lp_r.at[r], partner)

    def lo_product(r):
        lp_st[r] = dot(attn_all[r, mine(other), :], w_all[:, 0:split], 1, 0).astype(BF16)
        go(lo_pair(r))
        lo_own[r] = dot(attn_all[r, mine(q), :], w_all[:, 0:split], 1, 0)

    def lo_copy(r):
        return remote(lx_st.at[r - 1], lx_rx.at[r - 1], lx_s.at[r - 1], lx_r.at[r - 1],
                      device_at(xs[r], y, z, q))

    def lo_send(r):
        lo_pair(r).wait_recv()
        lx_st[r - 1] = (lo_own[r] + lp_rx[r].astype(F32)).astype(BF16)
        go(lo_copy(r))

    def lo_finish():
        lo_pair(0).wait_recv()
        out = lo_own[0] + lp_rx[0].astype(F32)
        for r in (1, 3, 2):
            lo_copy(r).wait_recv()
            out = out + lx_rx[r - 1].astype(F32)
        lo_ref[:, 0:split] = out.astype(BF16)

    def wy_copy(k):
        return remote(wg_st.at[ys[k]], wy_rx.at[k - 1], wy_s.at[k - 1], wy_r.at[k - 1],
                      device_at(x, ys[k], z, q))

    def wg_product():
        product = dot(attn_all[...].reshape(1024, HEAD),
                      og_all[...].reshape(1024, og_ref.shape[1]), 0, 0)
        for yy in range(4):
            for zz in range(4):
                wg_st[yy, zz * 16 : zz * 16 + 16, :] = product[
                    (zz * 4 + yy) * 16 : (zz * 4 + yy) * 16 + 16, :
                ].astype(BF16)
        for k in (1, 3, 2):
            go(wy_copy(k))

    def to_z(i):
        return remote(wsum.at[i], wz_rx.at[zh], wz_s.at[i], wz_r.at[zh],
                      device_at(x, y, i * 2 + q, zl))

    def wg_rows():
        total = wg_st[y].astype(F32)
        for k in (1, 3, 2):
            wy_copy(k).wait_recv()
            total = total + wy_rx[k - 1].astype(F32)
        wsum[...] = total.astype(BF16).reshape(4, 16, total.shape[-1])
        for i in range(4):
            here = (i == zh) & (zl == q)

            @pl.when(jnp.logical_not(here))
            def _():
                to_z(i).start()

            @pl.when(here)
            def _():
                wz_rx[zh] = wsum[i]

    def wp_copy():
        return remote(wp_st.at[other], wp_rx, wp_s, wp_r, partner)

    def wg_swap():
        for i in range(4):
            here = (i == zh) & (zl == q)

            @pl.when(jnp.logical_not(here))
            def _():
                remote(wsum.at[0], wz_rx.at[i], wz_s.at[0], wz_r.at[i], partner).wait_recv()

        rows = jnp.sum(wz_rx[...].astype(F32), axis=0)
        wp_st[...] = rows.reshape(2, 8, rows.shape[-1])
        go(wp_copy())

    def wg_finish():
        wp_copy().wait_recv()
        wg_ref[...] = (wp_st[q] + wp_rx[...]) * normaliser

    def dq_copy():
        return remote(dq_st.at[:, mine(other)], dq_rx, dqs, dqr, partner)

    def dq_finish():
        dq_mine = dq_st[:, mine(q), :]
        dq_copy().wait_recv()
        for h in range(4):
            dq_ref[:, lanes(q * 4 + h)] = dq_mine[h]
            dq_ref[:, lanes(other * 4 + h)] = dq_rx[h]

    og_forward(1)
    og_forward(3)
    og_far = 3 - 2 * q
    og_cp[2] = go(remote(og_all.at[og_far, mine(q)], og_all.at[2, mine(q)], og_s.at[2],
                         og_r.at[2], device_at(lax.rem(x + 5 - 2 * q, 4), y, z, q)))
    relay(0)
    weight_wait()
    head_gradient(1)
    head_gradient(3)
    head_gradient(0)
    query_wait()
    og_forward(2)
    head_gradient(2)
    wx_send()
    window_wait(0)
    forward(0)
    relay(1)
    backward(0)
    window_wait(1)
    forward(1)
    relay_sums(0)
    backward(1)
    go(dq_copy())
    attn_wait()
    wg_product()
    for r in (1, 3, 2, 0):
        lo_product(r)
    for r in (1, 3, 2):
        lo_send(r)
    relay_sums(1)
    tail_product()
    dq_finish()
    own_sums(0)
    own_sums(1)
    wg_rows()
    tail_finish()
    wg_swap()
    lo_finish()
    own_finish(0)
    wg_finish()
    own_finish(1)

    for copy in sends:
        copy.wait_send()
    up_z(0).wait_send()
    up_z(1).wait_send()
    for m in range(2):
        for k in range(1, 4):
            for half in range(2):
                along_y(m, k, half, own_st).wait_send()
    for h in range(4):
        @pl.when(x != h)
        def _():
            attn_copy(h).wait_send()
    for i in range(4):
        @pl.when(jnp.logical_not((i == zh) & (zl == q)))
        def _():
            to_z(i).wait_send()

    for m in range(2):
        @pl.when(q == 1)
        def _():
            remote(zbuf.at[m, 0], win.at[m, pl.ds(0, BLOCK)], p0_s.at[m], p0_r.at[m],
                   partner).wait_send()

        @pl.when(q == 0)
        def _():
            remote(dkv.at[m, pl.ds(0, BLOCK)], d4_rx.at[m], d4s.at[m], d4r.at[m],
                   partner).wait_send()


def hand_over(*refs):
    for src, dst in zip(refs[:5], refs[5:]):
        dst[...] = src[...]


def per_device(query, keys, values, out_weight, out_grad, doc_blocks):
    width = out_grad.shape[2]
    tokens = lax.axis_size("dp") * lax.axis_size("seq") * BLOCK
    vmem = pl.BlockSpec(memory_space=pltpu.VMEM)
    dma = pltpu.SemaphoreType.DMA
    scratch = [
        ((2, 2, BLOCK, 512), BF16),
        ((2, 2, BLOCK, 512), BF16),
        ((2, ROWS, 512), BF16),
        ((256, 1024), BF16),
        ((4, 256, width), BF16),
        ((HEAD, width), BF16),
        ((3, 256, HEAD), BF16),
        ((4, 256, HEAD), BF16),
        ((256, ROWS), F32),
        ((2, 256, ROWS), F32),
        ((4, 256, HEAD), BF16),
        ((4, 256, HEAD), BF16),
        ((4, 256, HEAD), BF16),
        ((4, BLOCK, HEAD), BF16),
        ((2, ROWS, 512), BF16),
        ((2, BLOCK, 512), BF16),
        ((2, BLOCK, 512), BF16),
        ((2, 3, 2, BLOCK, 512), BF16),
        ((2, 2, BLOCK, 512), F32),
        ((2, 2, BLOCK, 512), BF16),
        ((2, 2, BLOCK, 512), BF16),
        ((4, 64, width), BF16),
        ((3, 64, width), BF16),
        ((4, 16, width), BF16),
        ((4, 16, width), BF16),
        ((2, 8, width), F32),
        ((8, width), F32),
        ((4, BLOCK, SPLIT), BF16),
        ((4, BLOCK, SPLIT), BF16),
        ((4, BLOCK, SPLIT), F32),
        ((3, BLOCK, SPLIT), BF16),
        ((3, BLOCK, SPLIT), BF16),
        ((4, HEAD, width - SPLIT), BF16),
        ((BLOCK, width - SPLIT), F32),
        ((BLOCK, width - SPLIT), F32),
        ((BLOCK, width - SPLIT), F32),
    ]
    semaphores = [
        (2,), (4,), (4,), (4,), (4,), (), (2,), (2,), (2,), (2, 3, 2), (2, 3, 2),
        (2,), (2,), (2,), (2,), (3,), (4,), (4,), (4,), (), (), (2,), (2,), (2,), (2,),
        (2, 3, 2), (2, 3, 2), (2,), (2,),
        (3,), (3,), (4,), (4,), (), (), (4,), (4,), (3,), (3,),
        (3,), (4,), (), (),
    ]
    results = pl.pallas_call(
        functools.partial(kernel, tokens ** (-0.5)),
        out_shape=[
            jax.ShapeDtypeStruct((BLOCK, width), BF16),
            jax.ShapeDtypeStruct((BLOCK, 2048), BF16),
            jax.ShapeDtypeStruct((BLOCK, 1024), BF16),
            jax.ShapeDtypeStruct((BLOCK, 1024), BF16),
            jax.ShapeDtypeStruct((8, width), F32),
        ],
        in_specs=[pl.BlockSpec(memory_space=pltpu.SMEM)] + [vmem] * 5,
        out_specs=[vmem] * 5,
        scratch_shapes=[pltpu.VMEM(*a) for a in scratch]
        + [dma(a) if a else dma for a in semaphores],
        compiler_params=pltpu.CompilerParams(
            collective_id=0, has_side_effects=True, vmem_limit_bytes=60 << 20
        ),
    )(doc_blocks, query[0], keys[0], values[0], out_weight, out_grad[0])
    results = pl.pallas_call(
        hand_over,
        out_shape=[jax.ShapeDtypeStruct(a.shape, a.dtype) for a in results],
        in_specs=[vmem] * 5,
        out_specs=[vmem] * 5,
        compiler_params=pltpu.CompilerParams(vmem_limit_bytes=60 << 20),
    )(*results)
    return tuple(a[None] for a in results[:4]) + (results[4],)


def solution(mesh):
    tokens = P("dp", "seq", None)
    return jax.shard_map(
        per_device,
        mesh=mesh,
        in_specs=(tokens, tokens, tokens, P("dp", None), tokens, P("dp", None)),
        out_specs=(tokens, tokens, tokens, tokens, P(("dp", "seq"), None)),
        check_vma=False,
    )
```

time: 122 us -> 97.5 us (0.80)
  the two profiles are of different devices: /device:TPU:53 before, /device:TPU:1 now
where the time goes in v2:
time: 97.5 us; the launch traced here: 97.1 us
  Pallas kernels  96.5 us (99%)
    pallas_call x1, Pallas kernels, per_device(): pl.pallas_call(functools.partial(kernel, tokens ** (-0.5)), out_shape=[ja...  94 us
    pallas_call x1, Pallas kernels, per_device(): pl.pallas_call(hand_over, out_shape=[jax.ShapeDtypeStruct(a.shape, a.dtyp...  2.5 us

profile of v2, /device:TPU:1, one launch (start us, length us, event | category | flops | bytes accessed | tf_op | source)
XLA Modules:
  0.0 97.1 jit_solution(16230328396796907800)
XLA Ops:
  0.6 94.0 %shard_map.101 = (bf16[128,1920]{1,0:T(8,128)(2,1)}, bf16[128,2048]{1,0:T(8,128)(2,1)}, bf16[128,1024]{1,0:T(8,128)(2,1)}, bf16[128,1024]{1,0:T(8,128)(2,1)}, f32[8,1920]{1,0:T(8,128)}) custom-call(s32[1,8]{1,0:T(1,128)} %doc_ref.1, bf16[128,2048]{1,0:T(8,128)(2,1)} %bitcast.8, bf16[128,1024]{1,0:T(8,128)(2,1)} %bitcast.10, bf16[128,1024]{1,0:T(8,128)(2,1)} %bitcast.11, ...), custom_call_target="tpu_custom_call" | custom-call | tf_op jit(solution)/shard_map/pallas_call | solution.py:552
  94.6 2.5 %shard_map.102 = (bf16[128,1920]{1,0:T(8,128)(2,1)}, bf16[128,2048]{1,0:T(8,128)(2,1)}, bf16[128,1024]{1,0:T(8,128)(2,1)}, bf16[128,1024]{1,0:T(8,128)(2,1)}, f32[8,1920]{1,0:T(8,128)}) custom-call(bf16[128,1920]{1,0:T(8,128)(2,1)} %get-tuple-element.15.refs_0_, bf16[128,2048]{1,0:T(8,128)(2,1)} %get-tuple-element.16.refs_1_, ...), custom_call_target="tpu_custom_call" | custom-call | tf_op jit(solution)/shard_map/pallas_call | solution.py:569

commit v3 on v2

--- a/solution.py
+++ b/solution.py
@@ -91,22 +91,25 @@
         sends.append(copy)
         return copy
 
-    def up_z(m):
-        return remote(own_st.at[m], zbuf.at[m], zk_s.at[m], zk_r.at[m],
+    def up_z(c):
+        m, lo, rows = ((0, 0, BLOCK), (1, 0, 64), (1, 64, 64))[c]
+        rows = pl.ds(lo, rows)
+        return remote(own_st.at[m, :, rows], zbuf.at[m, :, rows], zk_s.at[c], zk_r.at[c],
                       device_at(x, y, lax.rem(z + 2, 8), q))
 
-    def along_y(m, k, half, src):
+    def along_y(m, k, half, src, lo=0, rows=BLOCK):
+        first = pl.multiple_of((7 - 2 * k + q) * BLOCK + lo, 64)
         return remote(
-            src.at[m, half], win.at[m, mine(7 - 2 * k + q)], yk_s.at[m, k - 1, half],
-            yk_r.at[m, k - 1, q], device_at(x, ys[k], z, half),
+            src.at[m, half, pl.ds(lo, rows)], win.at[m, pl.ds(first, rows)],
+            yk_s.at[m, k - 1, half], yk_r.at[m, k - 1, q], device_at(x, ys[k], z, half),
         )
 
     def og_send(k):
         return go(remote(og_ref, og_all.at[4 - k, mine(q)], og_s.at[k], og_r.at[4 - k],
                          device_at(xs[k], y, z, q)))
 
-    up_z(0).start()
-    up_z(1).start()
+    for c in range(3):
+        up_z(c).start()
     og_cp = {1: og_send(1), 3: og_send(3)}
     for m in range(2):
         for k in range(1, 4):
@@ -145,13 +148,17 @@
     def _():
         w_all[...] = w_ref[...]
 
-    def relay(m):
-        up_z(m).wait_recv()
+    def relay(c):
+        m, lo, rows = ((0, 0, BLOCK), (1, 0, 64), (1, 64, 64))[c]
+        up_z(c).wait_recv()
         for k in range(1, 4):
             @pl.when(y + k >= 4)
             def _():
                 for half in range(2):
-                    along_y(m, k, half, zbuf).start()
+                    along_y(m, k, half, zbuf, lo, rows).start()
+
+        if c == 1:
+            return
 
         @pl.when(q == 1)
         def _():
@@ -218,6 +225,13 @@
             dkv.at[m, pl.ds((7 - 2 * k + j) * BLOCK, BLOCK)], dy_rx.at[m, k - 1, q],
             yd_s.at[m, k - 1, j], yd_r.at[m, k - 1, q], device_at(x, ys[4 - k], z, j))
 
+    def dy_row(m):
+        for k in (3, 2, 1):
+            @pl.when(y - k >= 0)
+            def _():
+                for j in range(2):
+                    dy_copy(m, k, j).start()
+
     def backward(m):
         dk = jnp.zeros((ROWS, HEAD), F32)
         dv = jnp.zeros((ROWS, HEAD), F32)
@@ -240,8 +254,13 @@
         dkv[m, :, HEAD:] = dv.astype(BF16)
 
         for k in (3, 2, 1):
-            for j in range(2):
-                go(dy_copy(m, k, j))
+            @pl.when(y - k < 0)
+            def _():
+                for j in range(2):
+                    dy_copy(m, k, j).start()
+
+        if m == 0:
+            dy_row(0)
 
         @pl.when(q == 0)
         def _():
@@ -336,10 +355,13 @@
     def lo_pair(r):
         return remote(lp_st.at[r], lp_rx.at[r], lp_s.at[r], lp_r.at[r], partner)
 
-    def lo_product(r):
-        lp_st[r] = dot(attn_all[r, mine(other), :], w_all[:, 0:split], 1, 0).astype(BF16)
-        go(lo_pair(r))
-        lo_own[r] = dot(attn_all[r, mine(q), :], w_all[:, 0:split], 1, 0)
+    def lo_product():
+        part = dot(attn_all[:, mine(other), :].reshape(512, HEAD), w_all[:, 0:split], 1, 0)
+        lp_st[...] = part.astype(BF16).reshape(4, BLOCK, split)
+        for r in (1, 3, 2, 0):
+            go(lo_pair(r))
+        part = dot(attn_all[:, mine(q), :].reshape(512, HEAD), w_all[:, 0:split], 1, 0)
+        lo_own[...] = part.reshape(4, BLOCK, split)
 
     def lo_copy(r):
         return remote(lx_st.at[r - 1], lx_rx.at[r - 1], lx_s.at[r - 1], lx_r.at[r - 1],
@@ -434,12 +456,13 @@
     head_gradient(3)
     head_gradient(0)
     query_wait()
+    relay(1)
     og_forward(2)
     head_gradient(2)
     wx_send()
     window_wait(0)
     forward(0)
-    relay(1)
+    relay(2)
     backward(0)
     window_wait(1)
     forward(1)
@@ -448,31 +471,35 @@
     go(dq_copy())
     attn_wait()
     wg_product()
-    for r in (1, 3, 2, 0):
-        lo_product(r)
+    lo_product()
     for r in (1, 3, 2):
         lo_send(r)
     relay_sums(1)
+    dy_row(1)
     tail_product()
     dq_finish()
     own_sums(0)
-    own_sums(1)
     wg_rows()
     tail_finish()
     wg_swap()
     lo_finish()
+    own_sums(1)
     own_finish(0)
     wg_finish()
     own_finish(1)
 
     for copy in sends:
         copy.wait_send()
-    up_z(0).wait_send()
-    up_z(1).wait_send()
+    for c in range(3):
+        up_z(c).wait_send()
     for m in range(2):
         for k in range(1, 4):
             for half in range(2):
                 along_y(m, k, half, own_st).wait_send()
+    for m in range(2):
+        for k in (3, 2, 1):
+            for j in range(2):
+                dy_copy(m, k, j).wait_send()
     for h in range(4):
         @pl.when(x != h)
         def _():
@@ -543,7 +570,7 @@
         ((BLOCK, width - SPLIT), F32),
     ]
     semaphores = [
-        (2,), (4,), (4,), (4,), (4,), (), (2,), (2,), (2,), (2, 3, 2), (2, 3, 2),
+        (2,), (4,), (4,), (4,), (4,), (), (2,), (3,), (3,), (2, 3, 2), (2, 3, 2),
         (2,), (2,), (2,), (2,), (3,), (4,), (4,), (4,), (), (), (2,), (2,), (2,), (2,),
         (2, 3, 2), (2, 3, 2), (2,), (2,),
         (3,), (3,), (4,), (4,), (), (), (4,), (4,), (3,), (3,),

time: 97.5 us -> 96.1 us (0.986)
  Pallas kernels: 96.5 us -> 95.3 us
    pallas_call x1, Pallas kernels: 94 us -> 92.8 us  [per_device(): pl.pallas_call(functools.partial(kernel, tokens ** (-0.5)), out_shape=[ja...]
where the time goes in v3:
time: 96.1 us; the launch traced here: 95.9 us
  Pallas kernels  95.3 us (99%)
    pallas_call x1, Pallas kernels, per_device(): pl.pallas_call(functools.partial(kernel, tokens ** (-0.5)), out_shape=[ja...  92.8 us
    pallas_call x1, Pallas kernels, per_device(): pl.pallas_call(hand_over, out_shape=[jax.ShapeDtypeStruct(a.shape, a.dtyp...  2.5 us

profile of v3, /device:TPU:1, one launch (start us, length us, event | category | flops | bytes accessed | tf_op | source)
XLA Modules:
  0.0 95.9 jit_solution(13057036292542441418)
XLA Ops:
  0.6 92.8 %shard_map.101 = (bf16[128,1920]{1,0:T(8,128)(2,1)}, bf16[128,2048]{1,0:T(8,128)(2,1)}, bf16[128,1024]{1,0:T(8,128)(2,1)}, bf16[128,1024]{1,0:T(8,128)(2,1)}, f32[8,1920]{1,0:T(8,128)}) custom-call(s32[1,8]{1,0:T(1,128)} %doc_ref.1, bf16[128,2048]{1,0:T(8,128)(2,1)} %bitcast.8, bf16[128,1024]{1,0:T(8,128)(2,1)} %bitcast.10, bf16[128,1024]{1,0:T(8,128)(2,1)} %bitcast.11, ...), custom_call_target="tpu_custom_call" | custom-call | tf_op jit(solution)/shard_map/pallas_call | solution.py:579
  93.4 2.5 %shard_map.102 = (bf16[128,1920]{1,0:T(8,128)(2,1)}, bf16[128,2048]{1,0:T(8,128)(2,1)}, bf16[128,1024]{1,0:T(8,128)(2,1)}, bf16[128,1024]{1,0:T(8,128)(2,1)}, f32[8,1920]{1,0:T(8,128)}) custom-call(bf16[128,1920]{1,0:T(8,128)(2,1)} %get-tuple-element.15.refs_0_, bf16[128,2048]{1,0:T(8,128)(2,1)} %get-tuple-element.16.refs_1_, ...), custom_call_target="tpu_custom_call" | custom-call | tf_op jit(solution)/shard_map/pallas_call | solution.py:596

commit v4 on v3

--- a/solution.py
+++ b/solution.py
@@ -12,7 +12,7 @@
 WINDOW = 1024
 SLOTS = 9
 ROWS = SLOTS * BLOCK
-SPLIT = 1152
+SPLIT = 1024
 MESH = pl.DeviceIdType.MESH
 F32 = jnp.float32
 BF16 = jnp.bfloat16

time: 96.1 us -> 100 us (1.041)
  Pallas kernels: 95.3 us -> 99.6 us
    pallas_call x1, Pallas kernels: 92.8 us -> 97.1 us  [per_device(): pl.pallas_call(functools.partial(kernel, tokens ** (-0.5)), out_shape=[ja...]
where the time goes in v4:
time: 100 us
  Pallas kernels  99.6 us (100%)
    pallas_call x1, Pallas kernels, per_device(): pl.pallas_call(functools.partial(kernel, tokens ** (-0.5)), out_shape=[ja...  97.1 us
    pallas_call x1, Pallas kernels, per_device(): pl.pallas_call(hand_over, out_shape=[jax.ShapeDtypeStruct(a.shape, a.dtyp...  2.5 us

profile of v4, /device:TPU:1, one launch (start us, length us, event | category | flops | bytes accessed | tf_op | source)
XLA Modules:
  0.0 100.2 jit_solution(5206477265024854777)
XLA Ops:
  0.6 97.1 %shard_map.101 = (bf16[128,1920]{1,0:T(8,128)(2,1)}, bf16[128,2048]{1,0:T(8,128)(2,1)}, bf16[128,1024]{1,0:T(8,128)(2,1)}, bf16[128,1024]{1,0:T(8,128)(2,1)}, f32[8,1920]{1,0:T(8,128)}) custom-call(s32[1,8]{1,0:T(1,128)} %doc_ref.1, bf16[128,2048]{1,0:T(8,128)(2,1)} %bitcast.8, bf16[128,1024]{1,0:T(8,128)(2,1)} %bitcast.10, bf16[128,1024]{1,0:T(8,128)(2,1)} %bitcast.11, ...), custom_call_target="tpu_custom_call" | custom-call | tf_op jit(solution)/shard_map/pallas_call | solution.py:579
  97.7 2.5 %shard_map.102 = (bf16[128,1920]{1,0:T(8,128)(2,1)}, bf16[128,2048]{1,0:T(8,128)(2,1)}, bf16[128,1024]{1,0:T(8,128)(2,1)}, bf16[128,1024]{1,0:T(8,128)(2,1)}, f32[8,1920]{1,0:T(8,128)}) custom-call(bf16[128,1920]{1,0:T(8,128)(2,1)} %get-tuple-element.15.refs_0_, bf16[128,2048]{1,0:T(8,128)(2,1)} %get-tuple-element.16.refs_1_, ...), custom_call_target="tpu_custom_call" | custom-call | tf_op jit(solution)/shard_map/pallas_call | solution.py:596
